TPU v7x, 128 devices: a whole 4x4x4 slice. The times are simulated.
128 devices in a mesh: section: 8 (over y, z_lo), dp: 16 (over z_hi, x, core).
Axes of the slice: x: 4, y: 4, z: 4 (z_hi: 2, z_lo: 2; z = z_hi * 2 + z_lo), core: 2. Of those that a mesh axis runs over, the one named last changes fastest.
Arguments:
- embedded: bfloat16 [8192, 1536], P('dp'), may hold values from -6 to 6
- hidden_out: bfloat16 [8, 8192, 1536], P('section', 'dp'), may hold values from -6 to 6
- out_grads: bfloat16 [8, 8192, 8192], P('section', 'dp'), may hold values from -6 to 6
- counts: int32 [16, 2], replicated, may hold values from 64 to 256, as said below
- owners: int32 [8, 12, 1], P('section'), may hold values from 0 to 15; in each aligned block of 12 rows (0 to 11, 12 to 23, ..., all dimensions but the last counted through in order) at most 2 rows name the same one
- ginv: bfloat16 [8, 64, 128, 128], P('section', 'dp'), as said below
- ainv: bfloat16 [8, 16, 2, 128, 128], P('section', 'dp'), as said below
Outputs:
- update: bfloat16 [8, 8192, 1536], P('section', 'dp')
Inputs may be any that keep to these rules, and one draw needn't show every extreme that they name: `counts`: every replica fills its slots from the front; in every draw some micro-batch is full with 256 valid tokens. `owners`: within one layer no replica holds more than 2 tiles, and in every draw some replica holds exactly 2 tiles of some layer. `ginv`: symmetric blocks. `ainv`: symmetric blocks; slots that no tile uses hold arbitrary values.
All inputs are finite; a program needn't handle non-finite values.
Results may differ from a plain program's by a relative error of at most 0.022.
Values may be sent and summed in bfloat16 or wider, within the bound.
A program may use at most 192 MiB of HBM per device.

v0:
```python
import jax
import jax.numpy as jnp
from jax import lax
from jax.sharding import PartitionSpec as P


def shifted(block, axis, distance):
    devices = range(lax.axis_size(axis))
    route = [(i - distance, i) for i in devices if i - distance in devices]
    return lax.ppermute(block, axis, route)


def local(embedded, hidden_out, out_grads, counts, owners, ginv, ainv):
    section_index = lax.axis_index("section")
    replica = lax.axis_index("dp")
    groups = lax.axis_size("dp")
    received = shifted(hidden_out[0], "section", 1)
    inputs = jnp.where(section_index == 0, embedded, received)
    micro_count = counts.shape[1]
    tok_rows, window = inputs.shape
    micro_rows = tok_rows // micro_count
    own_counts = lax.dynamic_index_in_dim(counts, replica, 0, keepdims=False)
    usable = (jnp.arange(micro_rows)[None, :] < own_counts[:, None]).reshape(tok_rows)
    token_scale = 1.0 / jnp.sqrt(jnp.sum(counts).astype(jnp.float32))
    masked = out_grads[0] * usable[:, None].astype(jnp.bfloat16)
    model_width = masked.shape[1]
    block_size = ginv.shape[-1]
    local_rows = model_width // groups
    grad_rows = lax.psum_scatter(
        (
            lax.dot_general(
                masked, inputs, (((0,), (0,)), ((), ())), preferred_element_type=jnp.float32
            )
            * token_scale
        ).astype(jnp.bfloat16),
        "dp",
        scatter_dimension=0,
        tiled=True,
    )
    gain_blocks = ginv[0]
    block_count = gain_blocks.shape[0]
    adjusted = jnp.einsum(
        "bij,bjw->biw",
        gain_blocks,
        grad_rows.reshape(block_count, block_size, window),
        preferred_element_type=jnp.float32,
    )
    adjusted = adjusted.astype(jnp.bfloat16).reshape(local_rows, window)
    tile_count = window // block_size
    owner_of = owners[0, :, 0]
    capacity = ainv.shape[2]
    tile_index = jnp.arange(tile_count)
    shared = owner_of[None, :] == owner_of[:, None]
    slot_of = jnp.sum(shared & (tile_index[None, :] < tile_index[:, None]), axis=1)
    picker = (
        (owner_of[None, None, :] == jnp.arange(groups)[:, None, None])
        & (slot_of[None, None, :] == jnp.arange(capacity)[None, :, None])
    ).astype(jnp.bfloat16)
    pieces = adjusted.reshape(local_rows, tile_count, block_size)
    factors = ainv[0, 0]
    factor_copies = lax.all_gather(factors, "dp", axis=0, tiled=True)
    chosen = jnp.einsum(
        "mt,mij->tij",
        picker.reshape(groups * capacity, tile_count),
        factor_copies,
        preferred_element_type=jnp.float32,
    ).astype(jnp.bfloat16)
    result = jnp.einsum("rtk,tkj->rtj", pieces, chosen, preferred_element_type=jnp.float32).astype(
        jnp.bfloat16
    )
    return result.reshape(local_rows, window)[None]


def solution(mesh):
    placed = (
        P("dp", None),
        P("section", "dp", None),
        P("section", "dp", None),
        P(),
        P("section", None, None),
        P("section", "dp", None, None),
        P("section", "dp", None, None, None),
    )
    return jax.shard_map(
        local, mesh=mesh, in_specs=placed, out_specs=P("section", "dp", None), check_vma=False
    )
```

profile of v0, /device:TPU:0, one launch (start us, length us, event | category | flops | bytes accessed | tf_op | source)
XLA Modules:
  0.0 292.5 jit_solution(1442240782451695092)
XLA Ops:
  6.5 0.0 copy-start
  6.5 0.0 all-gather.3.cloned.1.call-start
  6.5 4.1 %collective-permute-start = (bf16[512,1536]{1,0:T(8,128)(2,1)}, bf16[512,1536]{1,0:T(8,128)(2,1)S(1)}, u32[]{:S(2)}, u32[]{:S(2)}) collective-permute-start(bf16[512,1536]{1,0:T(8,128)(2,1)} %bitcast.34), channel_id=1, source_target_pairs={{0,16},{16,32},{32,48},{48,64},{64,80},{80,96},{96,112},{1,17},{17... | collective-permute-start | bytes 4718600 | tf_op jit(solution)/shard_map/ppermute | solution.py:10
  10.7 0.0 all-gather.3.cloned.1.call-update
  10.7 0.0 reduce-scatter.2.cloned.1.call-start
  10.8 1.3 reduce_sum.19
  12.1 0.9 dynamic-slice_reduce_fusion
  12.9 0.1 fusion.10
  13.7 31.5 %collective-permute-done = bf16[512,1536]{1,0:T(8,128)(2,1)S(1)} collective-permute-done((bf16[512,1536]{1,0:T(8,128)(2,1)}, bf16[512,1536]{1,0:T(8,128)(2,1)S(1)}, u32[]{:S(2)}, u32[]{:S(2)}) %collective-permute-start) | collective-permute-done | bytes 1572896 | tf_op jit(solution)/shard_map/ppermute | solution.py:10
  45.2 21.0 %multiply_convert_fusion = bf16[8192,1536]{1,0:T(8,128)(2,1)} fusion(f32[]{:T(128)S(6)} %sqrt.3, bf16[1,512,8192]{2,1,0:T(8,128)(2,1)} %param.9, bf16[512]{0:T(512)(128)(2,1)S(1)} %bitcast.31, bf16[512,1536]{1,0:T(8,128)(2,1)} %param.7, bf16[512,1536]{1,0:T(8,128)(2,1)S(1)} %collective-permute-done, pred[]{:T(512)S(6)} %eq.64), kind=kOutput, calls=%fused_computation | convolution fusion | flops 12915048448 | bytes 36701188 | tf_op jit(solution)/shard_map/dot_general | solution.py:31
  66.2 0.0 copy-start.1
  66.2 0.0 reduce-scatter.2.cloned.1.call-update
  66.2 0.6 copy-done.1
  66.9 0.2 convert_reduce_fusion
  67.1 11.5 %all-gather.3.cloned.1.call-done = bf16[1,1,32,128,128]{4,3,1,0,2:T(8,128)(2,1)} async-done(((bf16[1,1,2,128,128]{4,3,1,0,2:T(8,128)(2,1)}), bf16[1,1,32,128,128]{4,3,1,0,2:T(8,128)(2,1)}) %all-gather.3.cloned.1.call-update) | async-done | bytes 1048592 | tf_op jit(solution)/shard_map/all_gather | solution.py:61
  78.6 2.7 convolution_convert_fusion.2
  81.3 191.1 %reduce-scatter.2.cloned.1.call-done = bf16[512,1536]{1,0:T(8,128)(2,1)} async-done(((bf16[8192,1536]{1,0:T(8,128)(2,1)}), bf16[512,1536]{1,0:T(8,128)(2,1)}) %reduce-scatter.2.cloned.1.call-update) | async-done | bytes 1572880 | tf_op jit(solution)/shard_map/reduce_scatter | solution.py:29
  272.3 0.0 copy-done
  272.4 2.1 fusion.1
  274.5 7.3 %copy.26 = bf16[4,128,1536]{1,0,2:T(4,128)(2,1)S(1)} copy(bf16[4,128,1536]{1,2,0:T(8,128)(2,1)S(1)} %fusion.1) | data formatting | bytes 3145728 | tf_op jit(solution)/shard_map/convert_element_type | solution.py:48
  281.8 0.6 reshape_reshape.3
  282.5 1.7 convolution_convert_fusion.1
  284.1 1.6 copy.29
  (5 shorter events, 0.1 us)
Async XLA Ops:
  6.5 265.8 %copy-start = (bf16[1,4,128,128]{3,2,1,0:T(8,128)(2,1)S(1)}, bf16[1,4,128,128]{3,2,1,0:T(8,128)(2,1)}, u32[]{:S(2)}) copy-start(bf16[1,4,128,128]{3,2,1,0:T(8,128)(2,1)} %param.12) | copy-start | bytes 393220
  6.5 72.1 %all-gather.3.cloned.1.call-start = ((), (), s32[]{:S(2)}) async-start(), calls=%async_computation.2 | async-start | bytes 1114112 | tf_op jit(solution)/shard_map/all_gather | solution.py:61
  6.5 38.7 %collective-permute-start = (bf16[512,1536]{1,0:T(8,128)(2,1)}, bf16[512,1536]{1,0:T(8,128)(2,1)S(1)}, u32[]{:S(2)}, u32[]{:S(2)}) collective-permute-start(bf16[512,1536]{1,0:T(8,128)(2,1)} %bitcast.34), channel_id=1, source_target_pairs={{0,16},{16,32},{32,48},{48,64},{64,80},{80,96},{96,112},{1,17},{17... | collective-permute-start | bytes 4718600 | tf_op jit(solution)/shard_map/ppermute | solution.py:10
  10.7 261.7 %reduce-scatter.2.cloned.1.call-start = ((), (), s32[]{:S(2)}) async-start(), calls=%async_computation.1 | async-start | bytes 26738688 | tf_op jit(solution)/shard_map/reduce_scatter | solution.py:29
  66.2 0.7 copy-start.1
Sparse Core Ops, SparseCore 0:
  10.8 67.7 all-gather.2
  83.0 189.2 reduce-scatter.1
where the time goes:
time: 293 us
  waiting for transfers between devices  234 us (80%)
  matrix products  27.5 us (9%)
  between operations  14.1 us (5%)
  local copies, waits for them, and re-layouts  11.1 us (4%)
  starting transfers between devices  4.17 us (1%)
    reduce_scatter x1, waiting for transfers between devices, local(): lax.psum_scatter((lax.dot_general(masked, inputs, (((0,), (0,)), ((), ())...  191 us
    ppermute x1, waiting for transfers between devices, shifted(): return lax.ppermute(block, axis, route)  31.5 us
    dot_general x1, matrix products, local(): lax.dot_general(masked, inputs, (((0,), (0,)), ((), ())), preferred_eleme...  21 us
    all_gather x1, waiting for transfers between devices, local(): factor_copies = lax.all_gather(factors, 'dp', axis=0, tiled=True)  11.5 us
    convert_element_type x1, local copies, waits for them, and re-layouts, local(): adjusted = adjusted.astype(jnp.bfloat16).reshape(local_rows, window)  7.33 us
  transfers between devices with their start and end apart: 3, of which 3 were waited for; matrix products, arithmetic and copies ran while one was open for 9% of the time, Pallas kernels for 0%

commit v1 on v0

v1 whole, which is shorter than its diff:
```python
import functools

import jax
import jax.numpy as jnp
from jax import lax
from jax.experimental import pallas as pl
from jax.experimental.pallas import tpu as pltpu
from jax.sharding import PartitionSpec as P

MESH = pl.DeviceIdType.MESH
F32 = jnp.float32
BF16 = jnp.bfloat16

CW = 128
AHEAD = 4


def kernel(
    dims, emb, hid, og, counts, owners, ginv, ainv, out,
    a_buf, b_buf, bt, m1, r1, m2, r2, own, zs, zr, ag, obuf,
    a_loc, a_snd, a_rcv, b_snd, b_rcv, f_snd, f_rcv, m1_snd, m1_rcv, m2_snd, m2_rcv,
    z_snd, z_rcv, g_snd, g_rcv, o_sem,
):
    sections, nx, rows, tok, window = dims
    nc = window // CW
    s = lax.axis_index("section")
    dp = lax.axis_index("dp")
    zh, x, c = dp // (2 * nx), (dp // 2) % nx, dp % 2

    def at(dx=0, z=None, core=None):
        z = zh if z is None else z
        core = c if core is None else core
        return (s, (z * nx + (x + dx) % nx) * 2 + core)

    right, left, across = at(1), at(nx - 1), at(2)
    opposite, partner = at(z=1 - zh), at(core=1 - c)
    following, previous = ((s + 1) % sections, dp), ((s + sections - 1) % sections, dp)

    def remote(src, dst, snd, rcv, device):
        return pltpu.make_async_remote_copy(
            src_ref=src, dst_ref=dst, send_sem=snd, recv_sem=rcv,
            device_id=device, device_id_type=MESH,
        )

    def columns_of(z, dx, core):
        block = (z * nx + (x + dx) % nx) * 2 + core
        return pl.ds(pl.multiple_of(block * rows, rows), rows)

    def a_local(z, dx):
        q = z * nx + dx
        return pltpu.make_async_copy(
            og.at[0, :, columns_of(z, dx, c)], a_buf.at[q, pl.ds(0, tok), :], a_loc.at[q]
        )

    def a_remote(z, dx):
        q = z * nx + dx
        return remote(
            og.at[0, :, columns_of(z, dx, 1 - c)], a_buf.at[q, pl.ds(tok, tok), :],
            a_snd.at[q], a_rcv.at[q], partner,
        )

    def window_cols(j):
        return pl.ds(pl.multiple_of(j * CW, CW), CW)

    def b_local(j):
        return pltpu.make_async_copy(
            emb.at[:, window_cols(j)], b_buf.at[j, pl.ds(0, tok), :], b_rcv.at[j]
        )

    def b_remote(j):
        return remote(
            hid.at[0, :, window_cols(j)], b_buf.at[j, pl.ds(0, tok), :],
            b_snd.at[j], b_rcv.at[j], following,
        )

    def forward(j):
        return remote(
            b_buf.at[j, pl.ds(0, tok), :], b_buf.at[j, pl.ds(tok, tok), :],
            f_snd.at[j], f_rcv.at[j], partner,
        )

    def first(d, j):
        return remote(
            m1.at[d, j], r1.at[d, j], m1_snd.at[d, j], m1_rcv.at[d, j], left if d else right
        )

    def second(d, z, j):
        return remote(
            m2.at[d, z, j], r2.at[d, z, j], m2_snd.at[d, z, j], m2_rcv.at[d, z, j],
            left if d else right,
        )

    def last(j):
        return remote(zs.at[j], zr.at[j], z_snd.at[j], z_rcv.at[j], opposite)

    def factor_x(k):
        return remote(
            ag.at[c, zh, x], ag.at[c, zh, x], g_snd.at[k - 1], g_rcv.at[k - 1], at(k)
        )

    def factor_z():
        return remote(ag.at[c, zh], ag.at[c, zh], g_snd.at[3], g_rcv.at[3], opposite)

    def factor_c():
        return remote(ag.at[c], ag.at[c], g_snd.at[4], g_rcv.at[4], partner)

    def store(j):
        return pltpu.make_async_copy(obuf.at[j], out.at[0, :, window_cols(j)], o_sem.at[j])

    def send_b(j):
        @pl.when(s == 0)
        def _():
            b_local(j).start()

        @pl.when(s < sections - 1)
        def _():
            b_remote(j).start()

    def take_b(j):
        @pl.when(s == 0)
        def _():
            b_local(j).wait()

        @pl.when(s > 0)
        def _():
            b_remote(j).wait_recv()

        forward(j).start()

    def wait_a(*pairs):
        for z, dx in pairs:
            a_local(z, dx).wait()
            a_remote(z, dx).wait_recv()

    for z, dx in ((0, 2), (1, 2), (1, 1), (0, 3), (0, 1), (1, 3), (0, 0), (1, 0)):
        a_local(z, dx).start()
    barrier = pltpu.get_barrier_semaphore()
    neighbours = (right, left, across, opposite, partner, following, previous)
    for device in neighbours:
        pl.semaphore_signal(barrier, inc=1, device_id=device, device_id_type=MESH)
    ag[c, zh, x] = ainv[0, 0]
    pl.semaphore_wait(barrier, len(neighbours))

    send_b(0)
    for z, dx in ((0, 2), (1, 2), (1, 1), (0, 3), (0, 1), (1, 3)):
        a_remote(z, dx).start()
    for j in range(1, min(AHEAD, nc)):
        send_b(j)
    for k in range(1, nx):
        factor_x(k).start()
    take_b(0)
    for z, dx in ((0, 0), (1, 0)):
        a_remote(z, dx).start()

    def bounds(core):
        replica = (zh * nx + x) * 2 + core
        return counts[replica, 0], counts[replica, 1]

    limits = (*bounds(c), *bounds(1 - c))
    half = tok // 2

    def transpose_b(j):
        for p in range(4):
            piece = b_buf[j, pl.ds(p * half, half), :].astype(F32)
            slots = lax.broadcasted_iota(jnp.int32, piece.shape, 0)
            piece = jnp.where(slots < limits[p], piece, 0.0)
            bt[j, :, pl.ds(p * half, half)] = piece.T.astype(BF16)

    def term(j, q):
        return jnp.dot(bt[j], a_buf[q], preferred_element_type=F32)

    def finish(j):
        total = jnp.int32(0)
        for r in range(counts.shape[0]):
            for m in range(counts.shape[1]):
                total = total + counts[r, m]
        scale = 1.0 / jnp.sqrt(jnp.full((1, rows), total.astype(F32)))
        grad = ((own[j % 2] + zr[j].astype(F32)) * scale).astype(BF16)
        blocks = ginv.shape[1]
        size = ginv.shape[-1]
        adjusted = jnp.concatenate(
            [
                jnp.dot(grad[:, b * size:(b + 1) * size], ginv[0, b], preferred_element_type=F32)
                for b in range(blocks)
            ],
            axis=1,
        ).astype(BF16)
        for k in range(CW // size):
            t = j * (CW // size) + k
            owner = owners[0, t, 0]
            slot = jnp.int32(0)
            for t2 in range(window // size):
                slot = slot + jnp.where((owners[0, t2, 0] == owner) & (t2 < t), 1, 0)
            slot = jnp.minimum(slot, ainv.shape[2] - 1)
            factor = ag[owner % 2, owner // (2 * nx), (owner // 2) % nx, slot]
            piece = jnp.dot(
                factor, adjusted[k * size:(k + 1) * size, :], preferred_element_type=F32
            )
            obuf[j, :, pl.ds(k * size, size)] = piece.T.astype(BF16)
        store(j).start()

    def step(i, carry):
        @pl.when((i >= 2) & (i < nc + 2))
        def _():
            j = i - 2

            @pl.when(i == 2)
            def _():
                wait_a((0, 1), (1, 3))

            for d, q in ((0, 1), (1, nx + 3)):
                value = term(j, q)
                first(d, j).wait_recv()
                m2[d, d, j] = (value + r1[d, j].astype(F32)).astype(BF16)
                second(d, d, j).start()

        @pl.when(i < nc)
        def _():
            @pl.when(i == 0)
            def _():
                wait_a((0, 2), (1, 2))

            forward(i).wait_recv()
            transpose_b(i)
            for d, q in ((0, 2), (1, nx + 2)):
                m1[d, i] = term(i, q).astype(BF16)
                first(d, i).start()

        @pl.when((i >= 1) & (i < nc + 1))
        def _():
            @pl.when(i == 1)
            def _():
                wait_a((1, 1), (0, 3))

            j = i - 1
            for d, q in ((0, nx + 1), (1, 3)):
                m2[d, 1 - d, j] = term(j, q).astype(BF16)
                second(d, 1 - d, j).start()

        @pl.when(i + AHEAD < nc)
        def _():
            send_b(i + AHEAD)

        @pl.when(i + 1 < nc)
        def _():
            take_b(i + 1)

        @pl.when(i == 1)
        def _():
            for k in range(1, nx):
                factor_x(k).wait_recv()
            factor_z().start()

        @pl.when(i == 2)
        def _():
            factor_z().wait_recv()
            factor_c().start()

        @pl.when((i >= 2) & (i < nc + 2))
        def _():
            j = i - 2

            @pl.when(i == 2)
            def _():
                wait_a((0, 0), (1, 0))

            away = term(j, (1 - zh) * nx)
            mine = term(j, zh * nx)
            second(0, 1, j).wait_recv()
            second(1, 0, j).wait_recv()
            second(0, 0, j).wait_recv()
            second(1, 1, j).wait_recv()
            zs[j] = (
                away + r2[0, 1 - zh, j].astype(F32) + r2[1, 1 - zh, j].astype(F32)
            ).astype(BF16)
            last(j).start()
            own[j % 2] = mine + r2[0, zh, j].astype(F32) + r2[1, zh, j].astype(F32)

        @pl.when(i >= 3)
        def _():
            @pl.when(i == 3)
            def _():
                factor_c().wait_recv()

            last(i - 3).wait_recv()
            finish(i - 3)

        return carry

    lax.fori_loop(0, nc + 3, step, 0)

    for z in range(2):
        for dx in range(nx):
            a_remote(z, dx).wait_send()
    for k in range(1, nx):
        factor_x(k).wait_send()
    factor_z().wait_send()
    factor_c().wait_send()

    def drain(j, carry):
        @pl.when(s < sections - 1)
        def _():
            b_remote(j).wait_send()

        forward(j).wait_send()
        for d in range(2):
            first(d, j).wait_send()
            for z in range(2):
                second(d, z, j).wait_send()
        last(j).wait_send()
        store(j).wait()
        return carry

    lax.fori_loop(0, nc, drain, 0)


def local(sections, groups, embedded, hidden_out, out_grads, counts, owners, ginv, ainv):
    tok, window = embedded.shape
    rows = out_grads.shape[-1] // groups
    nx = groups // 4
    nc = window // CW
    dims = (sections, nx, rows, tok, window)
    hbm = pl.BlockSpec(memory_space=pl.ANY)
    vmem = pl.BlockSpec(memory_space=pltpu.VMEM)
    smem = pl.BlockSpec(memory_space=pltpu.SMEM)
    dma = pltpu.SemaphoreType.DMA
    flops = 2 * tok * out_grads.shape[-1] * window
    return pl.pallas_call(
        functools.partial(kernel, dims),
        out_shape=jax.ShapeDtypeStruct((1, rows, window), BF16),
        in_specs=[hbm, hbm, hbm, smem, smem, vmem, vmem],
        out_specs=hbm,
        scratch_shapes=[
            pltpu.VMEM((2 * nx, 2 * tok, rows), BF16),
            pltpu.VMEM((nc, 2 * tok, CW), BF16),
            pltpu.VMEM((nc, CW, 2 * tok), BF16),
            pltpu.VMEM((2, nc, CW, rows), BF16),
            pltpu.VMEM((2, nc, CW, rows), BF16),
            pltpu.VMEM((2, 2, nc, CW, rows), BF16),
            pltpu.VMEM((2, 2, nc, CW, rows), BF16),
            pltpu.VMEM((2, CW, rows), F32),
            pltpu.VMEM((nc, CW, rows), BF16),
            pltpu.VMEM((nc, CW, rows), BF16),
            pltpu.VMEM((2, 2, nx) + ainv.shape[2:], BF16),
            pltpu.VMEM((nc, rows, CW), BF16),
            dma((2 * nx,)), dma((2 * nx,)), dma((2 * nx,)),
            dma((nc,)), dma((nc,)), dma((nc,)), dma((nc,)),
            dma((2, nc)), dma((2, nc)), dma((2, 2, nc)), dma((2, 2, nc)),
            dma((nc,)), dma((nc,)), dma((nx + 1,)), dma((nx + 1,)), dma((nc,)),
        ],
        compiler_params=pltpu.CompilerParams(
            collective_id=0, has_side_effects=True, vmem_limit_bytes=56 << 20
        ),
        cost_estimate=pl.CostEstimate(
            flops=flops, bytes_accessed=2 * out_grads.size, transcendentals=0
        ),
    )(embedded, hidden_out, out_grads, counts, owners, ginv, ainv)


def solution(mesh):
    placed = (
        P("dp", None),
        P("section", "dp", None),
        P("section", "dp", None),
        P(),
        P("section", None, None),
        P("section", "dp", None, None),
        P("section", "dp", None, None, None),
    )
    return jax.shard_map(
        functools.partial(local, mesh.shape["section"], mesh.shape["dp"]),
        mesh=mesh, in_specs=placed, out_specs=P("section", "dp", None), check_vma=False,
    )
```

time: 293 us -> 138 us (0.47)
  the two profiles are of different devices: /device:TPU:0 before, /device:TPU:40 now
where the time goes in v1:
time: 138 us; the launch traced here: 137 us
  Pallas kernels  132 us (96%)
  local copies, waits for them, and re-layouts  5.34 us (4%)
    pallas_call x1, Pallas kernels, local(): pl.pallas_call(functools.partial(kernel, dims), out_shape=jax.ShapeDtypeS...  132 us
    unnamed x3, local copies, waits for them, and re-layouts  5.34 us

profile of v1, /device:TPU:40, one launch (start us, length us, event | category | flops | bytes accessed | tf_op | source)
XLA Modules:
  0.0 137.3 jit_solution(18186836593618068224)
XLA Ops:
  0.0 1.4 copy.8.counts
  1.4 1.3 copy.9.owners
  2.7 132.0 %shard_map.73 = bf16[1,512,1536]{2,1,0:T(8,128)(2,1)} custom-call(bf16[512,1536]{1,0:T(8,128)(2,1)} %emb.1, bf16[1,512,1536]{2,1,0:T(8,128)(2,1)} %hid.1, bf16[1,512,8192]{2,1,0:T(8,128)(2,1)} %og.1, s32[16,2]{1,0:T(8,128)} %copy.8.counts, s32[1,12,1]{2,1,0:T(8,128)} %copy.9.owners, bf16[1,4,128,128]{3,2,1,0:T(8,128)(2,1)} %ginv.1, ...), custom_call_target="tpu_custom_call" | custom-call | flops 12884901888 | bytes 8388608 | tf_op jit(solution)/shard_map/pallas_call | solution.py:328
  134.7 2.7 %copy.11 = bf16[1,512,1536]{2,1,0:T(8,128)(2,1)} copy(bf16[1,512,1536]{2,1,0:T(8,128)(2,1)} %shard_map.73) | data formatting | bytes 3145728

commit v2 on v1

v2 whole, which is shorter than its diff:
```python
import functools

import jax
import jax.numpy as jnp
from jax import lax
from jax.experimental import pallas as pl
from jax.experimental.pallas import tpu as pltpu
from jax.sharding import PartitionSpec as P

MESH = pl.DeviceIdType.MESH
F32 = jnp.float32
BF16 = jnp.bfloat16

SW = 128
SUBS = 2
CW = SUBS * SW
UW = 512
AHEAD = 4
LAG = 2
PACE = (2, 2, 1, 1, 1, 1)


def kernel(
    dims, emb, hid, og, counts_in, owners_in, ginv, ainv, out,
    counts, owners, a_buf, a2, b_buf, b2, bt, bt2, m1, r1, m2, r2, own, zs, zr,
    n1, s1, n2, s2, comb, own2, ag, chosen, obuf, obuf2, hbuf, tbuf,
    i_sem, l_sem, t_sem, a_loc, a_snd, a_rcv, c_loc, c_snd, c_rcv, b_snd, b_rcv, e_snd, e_rcv, f_snd, f_rcv,
    h_snd, h_rcv, m1_snd, m1_rcv, m2_snd, m2_rcv, n1_snd, n1_rcv, n2_snd, n2_rcv,
    z_snd, z_rcv, g_snd, g_rcv, o_sem, o2_sem,
):
    sections, nx, rows, tok, window = dims
    nc = window // CW
    ns = window // SW
    nu = window // UW
    uw = UW
    size = ginv.shape[-1]
    blocks = ginv.shape[1]
    tail = size
    main = rows - tail
    s = lax.axis_index("section")
    dp = lax.axis_index("dp")
    zh, x, c = dp // (2 * nx), (dp // 2) % nx, dp % 2

    def spot(dx=0, z=None, core=None):
        z = zh if z is None else z
        core = c if core is None else core
        return (z * nx + (x + dx) % nx) * 2 + core

    right, left, across = (s, spot(1)), (s, spot(nx - 1)), (s, spot(2))
    opposite, partner = (s, spot(z=1 - zh)), (s, spot(core=1 - c))
    diagonal = (s, spot(z=1 - zh, core=1 - c))
    following, previous = ((s + 1) % sections, dp), ((s + sections - 1) % sections, dp)
    following2, previous2 = (following[0], opposite[1]), (previous[0], opposite[1])

    def remote(src, dst, snd, rcv, device):
        return pltpu.make_async_remote_copy(
            src_ref=src, dst_ref=dst, send_sem=snd, recv_sem=rcv,
            device_id=device, device_id_type=MESH,
        )

    def main_of(z, dx, core):
        return pl.ds(pl.multiple_of(spot(dx, z, core) * rows, rows), main)

    def tail_of(z, dx, core):
        return pl.ds(pl.multiple_of(spot(dx, z, core) * rows + main, tail), tail)

    def a_local(z, dx):
        q = z * nx + dx
        return pltpu.make_async_copy(
            og.at[0, :, main_of(z, dx, c)], a_buf.at[q, pl.ds(0, tok), :], a_loc.at[q]
        )

    def a_remote(z, dx):
        q = z * nx + dx
        return remote(
            og.at[0, :, main_of(z, dx, 1 - c)], a_buf.at[q, pl.ds(tok, tok), :],
            a_snd.at[q], a_rcv.at[q], partner,
        )

    def tail_local(dx):
        return pltpu.make_async_copy(
            og.at[0, :, tail_of(zh, dx, c)], a2.at[dx, pl.ds(0, tok), :], c_loc.at[dx]
        )

    def tail_load(g, dx):
        z = zh if g == 0 else 1 - zh
        core = c if g == 1 else 1 - c
        return pltpu.make_async_copy(
            og.at[0, :, tail_of(z, dx, core)], tbuf.at[g, dx], t_sem.at[g, dx]
        )

    def tail_remote(g, dx):
        return remote(
            tbuf.at[g, dx], a2.at[dx, pl.ds((g + 1) * tok, tok), :],
            c_snd.at[g, dx], c_rcv.at[g, dx], (partner, opposite, diagonal)[g],
        )

    def window_cols(j, width=SW):
        return pl.ds(pl.multiple_of(j * width, width), width)

    def b_load(j):
        return pltpu.make_async_copy(hid.at[0, :, window_cols(j)], hbuf.at[j], l_sem.at[j])

    def b_load_first(j):
        return pltpu.make_async_copy(emb.at[:, window_cols(j)], hbuf.at[j], l_sem.at[j])

    def b_remote(j):
        return remote(
            hbuf.at[j], b_buf.at[j, pl.ds(0, tok), :],
            b_snd.at[j], b_rcv.at[j], following,
        )

    def e_remote(j):
        return remote(
            hbuf.at[j], b2.at[j, pl.ds(0, tok), :],
            e_snd.at[j], e_rcv.at[j], following2,
        )

    def forward(j):
        return remote(
            b_buf.at[j, pl.ds(0, tok), :], b_buf.at[j, pl.ds(tok, tok), :],
            f_snd.at[j], f_rcv.at[j], partner,
        )

    def forward2(j):
        return remote(
            b2.at[j, pl.ds(0, tok), :], b2.at[j, pl.ds(tok, tok), :],
            h_snd.at[j], h_rcv.at[j], partner,
        )

    def first(d, j, h):
        part = pl.ds(h * SW, SW)
        return remote(
            m1.at[d, j, part, :], r1.at[d, j, part, :],
            m1_snd.at[d, j, h], m1_rcv.at[d, j, h], left if d else right,
        )

    def second(d, z, j):
        return remote(
            m2.at[d, z, j], r2.at[d, z, j], m2_snd.at[d, z, j], m2_rcv.at[d, z, j],
            left if d else right,
        )

    def first2(d, u):
        return remote(
            n1.at[d, u], s1.at[d, u], n1_snd.at[d, u], n1_rcv.at[d, u], left if d else right
        )

    def second2(d, h, u):
        return remote(
            n2.at[d, h, u], s2.at[d, h, u], n2_snd.at[d, h, u], n2_rcv.at[d, h, u],
            left if d else right,
        )

    def last(j):
        return remote(zs.at[j], zr.at[j], z_snd.at[j], z_rcv.at[j], opposite)

    def factor_x(own_z, k):
        z = zh if own_z else 1 - zh
        n = (0 if own_z else nx - 1) + k - 1
        return remote(ag.at[c, z, x], ag.at[c, z, x], g_snd.at[n], g_rcv.at[n], (s, spot(k)))

    def factor_z():
        n = 2 * nx - 2
        return remote(ag.at[c, zh, x], ag.at[c, zh, x], g_snd.at[n], g_rcv.at[n], opposite)

    def factor_c():
        n = 2 * nx - 1
        return remote(ag.at[c], ag.at[c], g_snd.at[n], g_rcv.at[n], partner)

    def store(j):
        return pltpu.make_async_copy(
            obuf.at[j], out.at[0, pl.ds(0, main), window_cols(j, CW)], o_sem.at[j]
        )

    def store2(j):
        return pltpu.make_async_copy(
            obuf2.at[j], out.at[0, pl.ds(main, tail), window_cols(j)], o2_sem.at[j]
        )

    def send_b(j):
        b_load(j).wait()
        b_remote(j).start()

    def take_b(j):
        b_remote(j).wait_recv()
        forward(j).start()
        e_remote(j).start()

    def take_b2(j):
        e_remote(j).wait_recv()
        forward2(j).start()

    def wait_a(*pairs):
        for z, dx in pairs:
            a_local(z, dx).wait()
            a_remote(z, dx).wait_recv()

    load_counts = pltpu.make_async_copy(counts_in, counts, i_sem.at[0])
    load_owners = pltpu.make_async_copy(owners_in, owners, i_sem.at[1])
    def load_b(j, carry):
        @pl.when(s == sections - 1)
        def _():
            b_load_first(j).start()

        @pl.when(s < sections - 1)
        def _():
            b_load(j).start()

        return carry

    lax.fori_loop(0, ns, load_b, 0)
    load_counts.start()
    load_owners.start()
    for z, dx in ((0, 2), (1, 2), (1, 1), (0, 3), (0, 1), (1, 3), (0, 0), (1, 0)):
        a_local(z, dx).start()
    for dx in range(nx):
        tail_local(dx).start()
        for g in range(3):
            tail_load(g, dx).start()
    barrier = pltpu.get_barrier_semaphore()
    neighbours = (
        right, left, across, opposite, partner, diagonal, following, previous, following2, previous2
    )
    for device in neighbours:
        pl.semaphore_signal(barrier, inc=1, device_id=device, device_id_type=MESH)
    ag[c, zh, x] = ainv[0, 0]
    pl.semaphore_wait(barrier, len(neighbours))

    send_b(0)
    factor_z().start()
    for z, dx in ((0, 2), (1, 2), (1, 1), (0, 3), (0, 1), (1, 3)):
        a_remote(z, dx).start()
    for k in range(1, nx):
        factor_x(True, k).start()
    for j in range(1, AHEAD):
        send_b(j)
    load_counts.wait()
    load_owners.wait()
    take_b(0)
    for z, dx in ((0, 0), (1, 0)):
        a_remote(z, dx).start()
    for dx in range(nx):
        tail_load(0, dx).wait()
        tail_remote(0, dx).start()

    def bounds(z, core):
        replica = spot(0, z, core)
        return counts[0, replica], counts[1, replica]

    half = tok // 2

    def transpose(source, target, j, z):
        limits = (*bounds(z, c), *bounds(z, 1 - c))
        for p in range(4):
            piece = source[j, pl.ds(p * half, half), :].astype(F32)
            slots = lax.broadcasted_iota(jnp.int32, piece.shape, 0)
            piece = jnp.where(slots < limits[p], piece, 0.0)
            target[window_cols(j), pl.ds(p * half, half)] = piece.T.astype(BF16)

    def term(j, q):
        return jnp.dot(bt[window_cols(j, CW), :], a_buf[q], preferred_element_type=F32)

    def scale(width):
        total = jnp.int32(0)
        for r in range(counts.shape[0]):
            for m in range(counts.shape[1]):
                total = total + counts[r, m]
        return 1.0 / jnp.sqrt(jnp.full((1, width), total.astype(F32)))

    def choose(t, carry):
        owner = owners[0, t]
        slot = jnp.int32(0)
        for t2 in range(window // size):
            slot = slot + jnp.where((owners[0, t2] == owner) & (t2 < t), 1, 0)
        slot = jnp.minimum(slot, ainv.shape[2] - 1)
        chosen[t] = ag[owner % 2, owner // (2 * nx), (owner // 2) % nx, slot]
        return carry

    def finish(j):
        last(j).wait_recv()
        grad = ((own[j] + zr[j].astype(F32)) * scale(main)).astype(BF16)
        adjusted = jnp.concatenate(
            [
                jnp.dot(grad[:, b * size:(b + 1) * size], ginv[0, b], preferred_element_type=F32)
                for b in range(blocks - 1)
            ],
            axis=1,
        ).astype(BF16)
        for k in range(CW // size):
            piece = jnp.dot(
                chosen[j * (CW // size) + k], adjusted[k * size:(k + 1) * size, :],
                preferred_element_type=F32,
            )
            obuf[j, :, pl.ds(k * size, size)] = piece.T.astype(BF16)
        store(j).start()

    def finish2(u, carry):
        for d in range(2):
            for h in range(2):
                second2(d, h, u).wait_recv()
        weights = scale(tail)
        grad = jnp.concatenate(
            [
                ((own2[u, h] + s2[0, h, u].astype(F32) + s2[1, h, u].astype(F32)) * weights)
                .astype(BF16)
                for h in range(2)
            ],
            axis=0,
        )
        adjusted = jnp.dot(grad, ginv[0, blocks - 1], preferred_element_type=F32).astype(BF16)
        for k in range(uw // size):
            t = u * (uw // size) + k
            piece = jnp.dot(
                chosen[t], adjusted[k * size:(k + 1) * size, :], preferred_element_type=F32
            )
            obuf2[t] = piece.T.astype(BF16)
            store2(t).start()
        return carry

    hw = uw // 2

    def begin2(u, carry):
        cols = pl.ds(pl.multiple_of(u * uw, uw), uw)
        near, far = bt[cols, :], bt2[cols, :]

        def side(start):
            return jnp.concatenate([a2[dx, pl.ds(start, 2 * tok), :] for dx in range(nx)], axis=1)

        value = jnp.dot(near, side(0), preferred_element_type=F32) + jnp.dot(
            far, side(2 * tok), preferred_element_type=F32
        )

        def block(h, dx):
            return value[h * hw:(h + 1) * hw, dx * tail:(dx + 1) * tail]

        for d in range(2):
            n1[d, u] = block(d, 2).astype(BF16)
            first2(d, u).start()
        for d, dx in ((0, 1), (1, nx - 1)):
            comb[d, u] = block(d, dx)
            n2[d, 1 - d, u] = block(1 - d, dx).astype(BF16)
        for h in range(2):
            own2[u, h] = block(h, 0)
        return carry

    def middle2(u, carry):
        for d in range(2):
            second2(d, 1 - d, u).start()
        for d in range(2):
            first2(d, u).wait_recv()
            n2[d, d, u] = (comb[d, u] + s1[d, u].astype(F32)).astype(BF16)
            second2(d, d, u).start()
        return carry

    def step(i, carry):
        @pl.when(i >= 2)
        def _():
            j = i - 2

            @pl.when(i == 2)
            def _():
                wait_a((0, 1), (1, 3))

            for d, q in ((0, 1), (1, nx + 3)):
                value = term(j, q)
                for h in range(SUBS):
                    first(d, j, h).wait_recv()
                m2[d, d, j] = (value + r1[d, j].astype(F32)).astype(BF16)
                second(d, d, j).start()

        @pl.when(i == 0)
        def _():
            wait_a((0, 2), (1, 2))
            for h in range(SUBS):
                if h:
                    take_b(h)
                forward(h).wait_recv()
                transpose(b_buf, bt, h, zh)
                for d, q in ((0, 2), (1, nx + 2)):
                    part = bt[pl.ds(h * SW, SW), :]
                    m1[d, 0, pl.ds(h * SW, SW), :] = jnp.dot(
                        part, a_buf[q], preferred_element_type=F32
                    ).astype(BF16)
                    first(d, 0, h).start()

        @pl.when((i > 0) & (i < nc))
        def _():
            for h in range(SUBS):
                forward(i * SUBS + h).wait_recv()
                transpose(b_buf, bt, i * SUBS + h, zh)
            for d, q in ((0, 2), (1, nx + 2)):
                m1[d, i] = term(i, q).astype(BF16)
                for h in range(SUBS):
                    first(d, i, h).start()

        @pl.when((i >= 1) & (i < nc + 1))
        def _():
            @pl.when(i == 1)
            def _():
                wait_a((1, 1), (0, 3))

            j = i - 1
            for d, q in ((0, nx + 1), (1, 3)):
                m2[d, 1 - d, j] = term(j, q).astype(BF16)
                second(d, 1 - d, j).start()

        @pl.when(i * SUBS + AHEAD < ns)
        def _():
            for h in range(SUBS):
                send_b(i * SUBS + AHEAD + h)

        pieces = [(g, dx) for g in (1, 2) for dx in range(nx)]
        for n, count in enumerate(PACE):
            @pl.when(i == n)
            def _():
                for g, dx in pieces[sum(PACE[:n]):sum(PACE[:n]) + count]:
                    tail_load(g, dx).wait()
                    tail_remote(g, dx).start()

        @pl.when(i + 1 < nc)
        def _():
            for h in range(SUBS):
                take_b((i + 1) * SUBS + h)

        @pl.when(i == 2)
        def _():
            factor_z().wait_recv()
            for k in range(1, nx):
                factor_x(False, k).start()

        @pl.when(i == 3)
        def _():
            for k in range(1, nx):
                factor_x(True, k).wait_recv()
                factor_x(False, k).wait_recv()
            factor_c().start()

        @pl.when((i >= 1) & (i < nc + 1))
        def _():
            for h in range(SUBS):
                forward2((i - 1) * SUBS + h).wait_recv()
                transpose(b2, bt2, (i - 1) * SUBS + h, 1 - zh)

        @pl.when(i == nc)
        def _():
            for dx in range(nx):
                tail_local(dx).wait()
                for g in range(3):
                    tail_remote(g, dx).wait_recv()
            lax.fori_loop(0, nu, begin2, 0)

        @pl.when(i == nc + 1)
        def _():
            lax.fori_loop(0, nu, middle2, 0)

        @pl.when(i >= 2)
        def _():
            j = i - 2

            @pl.when(i == 2)
            def _():
                wait_a((0, 0), (1, 0))

            away = term(j, (1 - zh) * nx)
            mine = term(j, zh * nx)
            second(0, 1, j).wait_recv()
            second(1, 0, j).wait_recv()
            second(0, 0, j).wait_recv()
            second(1, 1, j).wait_recv()
            zs[j] = (
                away + r2[0, 1 - zh, j].astype(F32) + r2[1, 1 - zh, j].astype(F32)
            ).astype(BF16)
            last(j).start()
            own[j] = mine + r2[0, zh, j].astype(F32) + r2[1, zh, j].astype(F32)

        @pl.when(i < nc)
        def _():
            for h in range(SUBS):
                take_b2(i * SUBS + h)

        @pl.when(i == 2 + LAG)
        def _():
            factor_c().wait_recv()
            lax.fori_loop(0, window // size, choose, 0)

        @pl.when(i >= 2 + LAG)
        def _():
            finish(i - 2 - LAG)

        return carry

    lax.fori_loop(0, nc + 2, step, 0)

    def rest(j, carry):
        finish(j)
        return carry

    lax.fori_loop(nc - LAG, nc, rest, 0)
    lax.fori_loop(0, nu, finish2, 0)

    for dx in range(nx):
        for z in range(2):
            a_remote(z, dx).wait_send()
        for g in range(3):
            tail_remote(g, dx).wait_send()
    for k in range(1, nx):
        factor_x(True, k).wait_send()
        factor_x(False, k).wait_send()
    factor_z().wait_send()
    factor_c().wait_send()

    def drain(j, carry):
        b_remote(j).wait_send()
        e_remote(j).wait_send()

        forward(j).wait_send()
        forward2(j).wait_send()
        store2(j).wait()
        return carry

    lax.fori_loop(0, ns, drain, 0)

    def drain1(j, carry):
        for d in range(2):
            for h in range(SUBS):
                first(d, j, h).wait_send()
            for z in range(2):
                second(d, z, j).wait_send()
        last(j).wait_send()
        store(j).wait()
        return carry

    lax.fori_loop(0, nc, drain1, 0)

    def drain2(u, carry):
        for d in range(2):
            first2(d, u).wait_send()
            for h in range(2):
                second2(d, h, u).wait_send()
        return carry

    lax.fori_loop(0, nu, drain2, 0)


def local(sections, groups, embedded, hidden_out, out_grads, counts, owners, ginv, ainv):
    tok, window = embedded.shape
    rows = out_grads.shape[-1] // groups
    size = ginv.shape[-1]
    main = rows - size
    nx = groups // 4
    nc, ns, nu = window // CW, window // SW, window // UW
    hw = UW // 2
    dims = (sections, nx, rows, tok, window)
    hbm = pl.BlockSpec(memory_space=pl.ANY)
    vmem = pl.BlockSpec(memory_space=pltpu.VMEM)
    dma = pltpu.SemaphoreType.DMA
    flops = 2 * tok * out_grads.shape[-1] * window
    return pl.pallas_call(
        functools.partial(kernel, dims),
        out_shape=jax.ShapeDtypeStruct((1, rows, window), BF16),
        in_specs=[hbm, hbm, hbm, hbm, hbm, vmem, vmem],
        out_specs=hbm,
        scratch_shapes=[
            pltpu.SMEM(counts.shape[::-1], jnp.int32),
            pltpu.SMEM(owners.shape[:2], jnp.int32),
            pltpu.VMEM((2 * nx, 2 * tok, main), BF16),
            pltpu.VMEM((nx, 4 * tok, size), BF16),
            pltpu.VMEM((ns, 2 * tok, SW), BF16),
            pltpu.VMEM((ns, 2 * tok, SW), BF16),
            pltpu.VMEM((window, 2 * tok), BF16),
            pltpu.VMEM((window, 2 * tok), BF16),
            pltpu.VMEM((2, nc, CW, main), BF16),
            pltpu.VMEM((2, nc, CW, main), BF16),
            pltpu.VMEM((2, 2, nc, CW, main), BF16),
            pltpu.VMEM((2, 2, nc, CW, main), BF16),
            pltpu.VMEM((nc, CW, main), F32),
            pltpu.VMEM((nc, CW, main), BF16),
            pltpu.VMEM((nc, CW, main), BF16),
            pltpu.VMEM((2, nu, hw, size), BF16),
            pltpu.VMEM((2, nu, hw, size), BF16),
            pltpu.VMEM((2, 2, nu, hw, size), BF16),
            pltpu.VMEM((2, 2, nu, hw, size), BF16),
            pltpu.VMEM((2, nu, hw, size), F32),
            pltpu.VMEM((nu, 2, hw, size), F32),
            pltpu.VMEM((2, 2, nx) + ainv.shape[2:], BF16),
            pltpu.VMEM((window // size, size, size), BF16),
            pltpu.VMEM((nc, main, CW), BF16),
            pltpu.VMEM((ns, size, SW), BF16),
            pltpu.VMEM((ns, tok, SW), BF16),
            pltpu.VMEM((3, nx, tok, size), BF16),
            dma((2,)), dma((ns,)), dma((3, nx)), dma((2 * nx,)), dma((2 * nx,)), dma((2 * nx,)),
            dma((nx,)), dma((3, nx)), dma((3, nx)),
            dma((ns,)), dma((ns,)), dma((ns,)), dma((ns,)), dma((ns,)), dma((ns,)),
            dma((ns,)), dma((ns,)),
            dma((2, nc, SUBS)), dma((2, nc, SUBS)), dma((2, 2, nc)), dma((2, 2, nc)),
            dma((2, nu)), dma((2, nu)), dma((2, 2, nu)), dma((2, 2, nu)),
            dma((nc,)), dma((nc,)), dma((2 * nx,)), dma((2 * nx,)), dma((nc,)), dma((ns,)),
        ],
        compiler_params=pltpu.CompilerParams(
            collective_id=0, has_side_effects=True, vmem_limit_bytes=60 << 20
        ),
        cost_estimate=pl.CostEstimate(
            flops=flops, bytes_accessed=2 * out_grads.size, transcendentals=0
        ),
    )(embedded, hidden_out, out_grads, counts.T, owners[:, :, 0], ginv, ainv)


def solution(mesh):
    placed = (
        P("dp", None),
        P("section", "dp", None),
        P("section", "dp", None),
        P(),
        P("section", None, None),
        P("section", "dp", None, None),
        P("section", "dp", None, None, None),
    )
    return jax.shard_map(
        functools.partial(local, mesh.shape["section"], mesh.shape["dp"]),
        mesh=mesh, in_specs=placed, out_specs=P("section", "dp", None), check_vma=False,
    )
```

time: 138 us -> 129 us (0.935)
  the two profiles are of different devices: /device:TPU:40 before, /device:TPU:0 now
where the time goes in v2:
time: 129 us
  Pallas kernels  126 us (98%)
  local copies, waits for them, and re-layouts  2.65 us (2%)
    pallas_call x1, Pallas kernels, local(): pl.pallas_call(functools.partial(kernel, dims), out_shape=jax.ShapeDtypeS...  126 us
    unnamed x1, local copies, waits for them, and re-layouts  2.65 us

profile of v2, /device:TPU:0, one launch (start us, length us, event | category | flops | bytes accessed | tf_op | source)
XLA Modules:
  0.0 128.9 jit_solution(2140532741037312923)
XLA Ops:
  0.0 126.2 %shard_map.73 = bf16[1,512,1536]{2,1,0:T(8,128)(2,1)} custom-call(bf16[512,1536]{1,0:T(8,128)(2,1)} %emb.1, bf16[1,512,1536]{2,1,0:T(8,128)(2,1)} %hid.1, bf16[1,512,8192]{2,1,0:T(8,128)(2,1)} %og.1, s32[2,16]{1,0:T(2,128)} %bitcast.2, s32[1,12]{1,0:T(1,128)} %bitcast.3, bf16[1,4,128,128]{3,2,1,0:T(8,128)(2,1)} %ginv.1, bf16[1,1,2,128,128]{4,3,2,1,0:T(8,128)(2,1)} %ainv.1), custom_call_target="tpu_custom_call" | custom-call | flops 12884901888 | bytes 8388608 | tf_op jit(solution)/shard_map/pallas_call | solution.py:559
  126.2 2.7 %copy.9 = bf16[1,512,1536]{2,1,0:T(8,128)(2,1)} copy(bf16[1,512,1536]{2,1,0:T(8,128)(2,1)} %shard_map.73) | data formatting | bytes 3145728

commit v3 on v2

--- a/solution.py
+++ b/solution.py
@@ -16,15 +16,17 @@
 CW = SUBS * SW
 UW = 512
 AHEAD = 4
-LAG = 2
+EARLY = 4
+PIECES2 = ((0, 2), (2, 6), (6, 10), (10, 12))
+LAG = 3
 PACE = (2, 2, 1, 1, 1, 1)
 
 
 def kernel(
     dims, emb, hid, og, counts_in, owners_in, ginv, ainv, out,
     counts, owners, a_buf, a2, b_buf, b2, bt, bt2, m1, r1, m2, r2, own, zs, zr,
-    n1, s1, n2, s2, comb, own2, ag, chosen, obuf, obuf2, hbuf, tbuf,
-    i_sem, l_sem, t_sem, a_loc, a_snd, a_rcv, c_loc, c_snd, c_rcv, b_snd, b_rcv, e_snd, e_rcv, f_snd, f_rcv,
+    n1, s1, n2, s2, comb, own2, ag, chosen, obuf, obuf2, hbuf, tbuf, relay,
+    i_sem, l_sem, t_sem, k_snd, k_rcv, a_loc, a_snd, a_rcv, c_loc, c_snd, c_rcv, b_snd, b_rcv, e_snd, e_rcv, f_snd, f_rcv,
     h_snd, h_rcv, m1_snd, m1_rcv, m2_snd, m2_rcv, n1_snd, n1_rcv, n2_snd, n2_rcv,
     z_snd, z_rcv, g_snd, g_rcv, o_sem, o2_sem,
 ):
@@ -50,7 +52,9 @@
     opposite, partner = (s, spot(z=1 - zh)), (s, spot(core=1 - c))
     diagonal = (s, spot(z=1 - zh, core=1 - c))
     following, previous = ((s + 1) % sections, dp), ((s + sections - 1) % sections, dp)
-    following2, previous2 = (following[0], opposite[1]), (previous[0], opposite[1])
+    even = s % 2 == 0
+    beside = (s // 2 * 2 + 1 - s % 2, opposite[1])
+    skipped, skipping = ((s + 2) % sections, dp), ((s + sections - 2) % sections, dp)
 
     def remote(src, dst, snd, rcv, device):
         return pltpu.make_async_remote_copy(
@@ -110,10 +114,17 @@
             b_snd.at[j], b_rcv.at[j], following,
         )
 
-    def e_remote(j):
-        return remote(
-            hbuf.at[j], b2.at[j, pl.ds(0, tok), :],
-            e_snd.at[j], e_rcv.at[j], following2,
+    def e_direct(j):
+        return remote(
+            hbuf.at[j], b2.at[j, pl.ds(0, tok), :], e_snd.at[j], e_rcv.at[j], beside
+        )
+
+    def e_relay(j):
+        return remote(hbuf.at[j], relay.at[j], e_snd.at[j], k_rcv.at[j], beside)
+
+    def e_pass(j):
+        return remote(
+            relay.at[j], b2.at[j, pl.ds(0, tok), :], k_snd.at[j], e_rcv.at[j], skipped
         )
 
     def forward(j):
@@ -179,16 +190,36 @@
         )
 
     def send_b(j):
-        b_load(j).wait()
         b_remote(j).start()
 
     def take_b(j):
         b_remote(j).wait_recv()
         forward(j).start()
-        e_remote(j).start()
+
+    def send_b2(j):
+        @pl.when(even)
+        def _():
+            e_direct(j).start()
+
+        @pl.when(jnp.logical_not(even))
+        def _():
+            e_relay(j).start()
+
+    def pass_b2(j):
+        @pl.when(even)
+        def _():
+            e_relay(j).wait_recv()
+            e_pass(j).start()
 
     def take_b2(j):
-        e_remote(j).wait_recv()
+        @pl.when(even)
+        def _():
+            e_pass(j).wait_recv()
+
+        @pl.when(jnp.logical_not(even))
+        def _():
+            e_direct(j).wait_recv()
+
         forward2(j).start()
 
     def wait_a(*pairs):
@@ -220,26 +251,36 @@
             tail_load(g, dx).start()
     barrier = pltpu.get_barrier_semaphore()
     neighbours = (
-        right, left, across, opposite, partner, diagonal, following, previous, following2, previous2
+        right, left, across, opposite, partner, diagonal, following, previous,
+        beside, skipped, skipping,
     )
     for device in neighbours:
         pl.semaphore_signal(barrier, inc=1, device_id=device, device_id_type=MESH)
     ag[c, zh, x] = ainv[0, 0]
     pl.semaphore_wait(barrier, len(neighbours))
 
+    b_load(0).wait()
     send_b(0)
     factor_z().start()
     for z, dx in ((0, 2), (1, 2), (1, 1), (0, 3), (0, 1), (1, 3)):
         a_remote(z, dx).start()
     for k in range(1, nx):
         factor_x(True, k).start()
-    for j in range(1, AHEAD):
+    send_b2(0)
+    for j in range(1, EARLY):
+        b_load(j).wait()
         send_b(j)
+        send_b2(j)
     load_counts.wait()
     load_owners.wait()
     take_b(0)
     for z, dx in ((0, 0), (1, 0)):
         a_remote(z, dx).start()
+    for j in range(EARLY, ns):
+        b_load(j).wait()
+        if j < AHEAD:
+            send_b(j)
+        send_b2(j)
     for dx in range(nx):
         tail_load(0, dx).wait()
         tail_remote(0, dx).start()
@@ -423,24 +464,25 @@
             for h in range(SUBS):
                 take_b((i + 1) * SUBS + h)
 
-        @pl.when(i == 2)
+        @pl.when(i == 3)
         def _():
             factor_z().wait_recv()
             for k in range(1, nx):
                 factor_x(False, k).start()
 
-        @pl.when(i == 3)
+        @pl.when(i == 4)
         def _():
             for k in range(1, nx):
                 factor_x(True, k).wait_recv()
                 factor_x(False, k).wait_recv()
             factor_c().start()
 
-        @pl.when((i >= 1) & (i < nc + 1))
-        def _():
-            for h in range(SUBS):
-                forward2((i - 1) * SUBS + h).wait_recv()
-                transpose(b2, bt2, (i - 1) * SUBS + h, 1 - zh)
+        for n, (low, high) in enumerate(PIECES2):
+            @pl.when(i == n + 3)
+            def _():
+                for j in range(low, high):
+                    forward2(j).wait_recv()
+                    transpose(b2, bt2, j, 1 - zh)
 
         @pl.when(i == nc)
         def _():
@@ -474,10 +516,16 @@
             last(j).start()
             own[j] = mine + r2[0, zh, j].astype(F32) + r2[1, zh, j].astype(F32)
 
-        @pl.when(i < nc)
-        def _():
-            for h in range(SUBS):
-                take_b2(i * SUBS + h)
+        for n, (low, high) in enumerate(PIECES2):
+            @pl.when(i == n + 1)
+            def _():
+                for j in range(low, high):
+                    pass_b2(j)
+
+            @pl.when(i == n + 2)
+            def _():
+                for j in range(low, high):
+                    take_b2(j)
 
         @pl.when(i == 2 + LAG)
         def _():
@@ -512,7 +560,16 @@
 
     def drain(j, carry):
         b_remote(j).wait_send()
-        e_remote(j).wait_send()
+
+        @pl.when(even)
+        def _():
+            e_direct(j).wait_send()
+            e_pass(j).wait_send()
+
+        @pl.when(jnp.logical_not(even))
+        def _():
+            e_relay(j).wait_send()
+
 
         forward(j).wait_send()
         forward2(j).wait_send()
@@ -589,7 +646,8 @@
             pltpu.VMEM((ns, size, SW), BF16),
             pltpu.VMEM((ns, tok, SW), BF16),
             pltpu.VMEM((3, nx, tok, size), BF16),
-            dma((2,)), dma((ns,)), dma((3, nx)), dma((2 * nx,)), dma((2 * nx,)), dma((2 * nx,)),
+            pltpu.VMEM((ns, tok, SW), BF16),
+            dma((2,)), dma((ns,)), dma((3, nx)), dma((ns,)), dma((ns,)), dma((2 * nx,)), dma((2 * nx,)), dma((2 * nx,)),
             dma((nx,)), dma((3, nx)), dma((3, nx)),
             dma((ns,)), dma((ns,)), dma((ns,)), dma((ns,)), dma((ns,)), dma((ns,)),
             dma((ns,)), dma((ns,)),

time: 129 us -> 121 us (0.938)
  Pallas kernels: 126 us -> 118 us
    pallas_call x1, Pallas kernels: 126 us -> 118 us  [local(): pl.pallas_call(functools.partial(kernel, dims), out_shape=jax.ShapeDtypeS...]
where the time goes in v3:
time: 121 us; the launch traced here: 120 us
  Pallas kernels  118 us (98%)
  local copies, waits for them, and re-layouts  2.65 us (2%)
    pallas_call x1, Pallas kernels, local(): pl.pallas_call(functools.partial(kernel, dims), out_shape=jax.ShapeDtypeS...  118 us
    unnamed x1, local copies, waits for them, and re-layouts  2.65 us

profile of v3, /device:TPU:0, one launch (start us, length us, event | category | flops | bytes accessed | tf_op | source)
XLA Modules:
  0.0 120.3 jit_solution(15024015926899556751)
XLA Ops:
  0.0 117.6 %shard_map.73 = bf16[1,512,1536]{2,1,0:T(8,128)(2,1)} custom-call(bf16[512,1536]{1,0:T(8,128)(2,1)} %emb.1, bf16[1,512,1536]{2,1,0:T(8,128)(2,1)} %hid.1, bf16[1,512,8192]{2,1,0:T(8,128)(2,1)} %og.1, s32[2,16]{1,0:T(2,128)} %bitcast.2, s32[1,12]{1,0:T(1,128)} %bitcast.3, bf16[1,4,128,128]{3,2,1,0:T(8,128)(2,1)} %ginv.1, bf16[1,1,2,128,128]{4,3,2,1,0:T(8,128)(2,1)} %ainv.1), custom_call_target="tpu_custom_call" | custom-call | flops 12884901888 | bytes 8388608 | tf_op jit(solution)/shard_map/pallas_call | solution.py:616
  117.6 2.7 %copy.9 = bf16[1,512,1536]{2,1,0:T(8,128)(2,1)} copy(bf16[1,512,1536]{2,1,0:T(8,128)(2,1)} %shard_map.73) | data formatting | bytes 3145728

commit v4 on v3

--- a/solution.py
+++ b/solution.py
@@ -18,7 +18,7 @@
 AHEAD = 4
 EARLY = 4
 PIECES2 = ((0, 2), (2, 6), (6, 10), (10, 12))
-LAG = 3
+LAG = 2
 PACE = (2, 2, 1, 1, 1, 1)
 
 
@@ -388,6 +388,9 @@
     def middle2(u, carry):
         for d in range(2):
             second2(d, 1 - d, u).start()
+        return carry
+
+    def end2(u, carry):
         for d in range(2):
             first2(d, u).wait_recv()
             n2[d, d, u] = (comb[d, u] + s1[d, u].astype(F32)).astype(BF16)
@@ -395,11 +398,11 @@
         return carry
 
     def step(i, carry):
-        @pl.when(i >= 2)
-        def _():
-            j = i - 2
-
-            @pl.when(i == 2)
+        @pl.when((i >= 1) & (i < nc + 1))
+        def _():
+            j = i - 1
+
+            @pl.when(i == 1)
             def _():
                 wait_a((0, 1), (1, 3))
 
@@ -428,6 +431,8 @@
         @pl.when((i > 0) & (i < nc))
         def _():
             for h in range(SUBS):
+                take_b(i * SUBS + h)
+            for h in range(SUBS):
                 forward(i * SUBS + h).wait_recv()
                 transpose(b_buf, bt, i * SUBS + h, zh)
             for d, q in ((0, 2), (1, nx + 2)):
@@ -435,16 +440,15 @@
                 for h in range(SUBS):
                     first(d, i, h).start()
 
-        @pl.when((i >= 1) & (i < nc + 1))
-        def _():
-            @pl.when(i == 1)
+        @pl.when(i < nc)
+        def _():
+            @pl.when(i == 0)
             def _():
                 wait_a((1, 1), (0, 3))
 
-            j = i - 1
             for d, q in ((0, nx + 1), (1, 3)):
-                m2[d, 1 - d, j] = term(j, q).astype(BF16)
-                second(d, 1 - d, j).start()
+                m2[d, 1 - d, i] = term(i, q).astype(BF16)
+                second(d, 1 - d, i).start()
 
         @pl.when(i * SUBS + AHEAD < ns)
         def _():
@@ -459,18 +463,13 @@
                     tail_load(g, dx).wait()
                     tail_remote(g, dx).start()
 
-        @pl.when(i + 1 < nc)
-        def _():
-            for h in range(SUBS):
-                take_b((i + 1) * SUBS + h)
-
-        @pl.when(i == 3)
+        @pl.when(i == 2)
         def _():
             factor_z().wait_recv()
             for k in range(1, nx):
                 factor_x(False, k).start()
 
-        @pl.when(i == 4)
+        @pl.when(i == 3)
         def _():
             for k in range(1, nx):
                 factor_x(True, k).wait_recv()
@@ -491,9 +490,6 @@
                 for g in range(3):
                     tail_remote(g, dx).wait_recv()
             lax.fori_loop(0, nu, begin2, 0)
-
-        @pl.when(i == nc + 1)
-        def _():
             lax.fori_loop(0, nu, middle2, 0)
 
         @pl.when(i >= 2)
@@ -516,6 +512,10 @@
             last(j).start()
             own[j] = mine + r2[0, zh, j].astype(F32) + r2[1, zh, j].astype(F32)
 
+        @pl.when(i == nc + 1)
+        def _():
+            lax.fori_loop(0, nu, end2, 0)
+
         for n, (low, high) in enumerate(PIECES2):
             @pl.when(i == n + 1)
             def _():
@@ -540,13 +540,49 @@
 
     lax.fori_loop(0, nc + 2, step, 0)
 
+    def drain(j, carry):
+        b_remote(j).wait_send()
+
+        @pl.when(even)
+        def _():
+            e_direct(j).wait_send()
+            e_pass(j).wait_send()
+
+        @pl.when(jnp.logical_not(even))
+        def _():
+            e_relay(j).wait_send()
+
+        forward(j).wait_send()
+        forward2(j).wait_send()
+        return carry
+
+    def drain1(j, carry):
+        for d in range(2):
+            for h in range(SUBS):
+                first(d, j, h).wait_send()
+            for z in range(2):
+                second(d, z, j).wait_send()
+        return carry
+
+    def drain2(u, carry):
+        for d in range(2):
+            first2(d, u).wait_send()
+            for h in range(2):
+                second2(d, h, u).wait_send()
+        return carry
+
+    def drain3(j, carry):
+        last(j).wait_send()
+        store(j).wait()
+        for h in range(SUBS):
+            store2(j * SUBS + h).wait()
+        return carry
+
     def rest(j, carry):
         finish(j)
         return carry
 
-    lax.fori_loop(nc - LAG, nc, rest, 0)
-    lax.fori_loop(0, nu, finish2, 0)
-
+    lax.fori_loop(nc - LAG, nc - 1, rest, 0)
     for dx in range(nx):
         for z in range(2):
             a_remote(z, dx).wait_send()
@@ -557,47 +593,12 @@
         factor_x(False, k).wait_send()
     factor_z().wait_send()
     factor_c().wait_send()
-
-    def drain(j, carry):
-        b_remote(j).wait_send()
-
-        @pl.when(even)
-        def _():
-            e_direct(j).wait_send()
-            e_pass(j).wait_send()
-
-        @pl.when(jnp.logical_not(even))
-        def _():
-            e_relay(j).wait_send()
-
-
-        forward(j).wait_send()
-        forward2(j).wait_send()
-        store2(j).wait()
-        return carry
-
     lax.fori_loop(0, ns, drain, 0)
-
-    def drain1(j, carry):
-        for d in range(2):
-            for h in range(SUBS):
-                first(d, j, h).wait_send()
-            for z in range(2):
-                second(d, z, j).wait_send()
-        last(j).wait_send()
-        store(j).wait()
-        return carry
-
     lax.fori_loop(0, nc, drain1, 0)
-
-    def drain2(u, carry):
-        for d in range(2):
-            first2(d, u).wait_send()
-            for h in range(2):
-                second2(d, h, u).wait_send()
-        return carry
-
+    finish(nc - 1)
+    lax.fori_loop(0, nu, finish2, 0)
     lax.fori_loop(0, nu, drain2, 0)
+    lax.fori_loop(0, nc, drain3, 0)
 
 
 def local(sections, groups, embedded, hidden_out, out_grads, counts, owners, ginv, ainv):

time: 121 us -> 118 us (0.975)
  Pallas kernels: 118 us -> 114 us
    pallas_call x1, Pallas kernels: 118 us -> 114 us  [local(): pl.pallas_call(functools.partial(kernel, dims), out_shape=jax.ShapeDtypeS...]
where the time goes in v4:
time: 118 us; the launch traced here: 116 us
  Pallas kernels  114 us (97%)
  local copies, waits for them, and re-layouts  2.65 us (2%)
    pallas_call x1, Pallas kernels, local(): pl.pallas_call(functools.partial(kernel, dims), out_shape=jax.ShapeDtypeS...  114 us
    unnamed x1, local copies, waits for them, and re-layouts  2.65 us

profile of v4, /device:TPU:0, one launch (start us, length us, event | category | flops | bytes accessed | tf_op | source)
XLA Modules:
  0.0 116.3 jit_solution(12326618761796681893)
XLA Ops:
  0.0 113.7 %shard_map.73 = bf16[1,512,1536]{2,1,0:T(8,128)(2,1)} custom-call(bf16[512,1536]{1,0:T(8,128)(2,1)} %emb.1, bf16[1,512,1536]{2,1,0:T(8,128)(2,1)} %hid.1, bf16[1,512,8192]{2,1,0:T(8,128)(2,1)} %og.1, s32[2,16]{1,0:T(2,128)} %bitcast.2, s32[1,12]{1,0:T(1,128)} %bitcast.3, bf16[1,4,128,128]{3,2,1,0:T(8,128)(2,1)} %ginv.1, bf16[1,1,2,128,128]{4,3,2,1,0:T(8,128)(2,1)} %ainv.1), custom_call_target="tpu_custom_call" | custom-call | flops 12884901888 | bytes 8388608 | tf_op jit(solution)/shard_map/pallas_call | solution.py:617
  113.7 2.7 %copy.9 = bf16[1,512,1536]{2,1,0:T(8,128)(2,1)} copy(bf16[1,512,1536]{2,1,0:T(8,128)(2,1)} %shard_map.73) | data formatting | bytes 3145728

commit v5 on v4

--- a/solution.py
+++ b/solution.py
@@ -166,17 +166,16 @@
     def last(j):
         return remote(zs.at[j], zr.at[j], z_snd.at[j], z_rcv.at[j], opposite)
 
-    def factor_x(own_z, k):
-        z = zh if own_z else 1 - zh
-        n = (0 if own_z else nx - 1) + k - 1
-        return remote(ag.at[c, z, x], ag.at[c, z, x], g_snd.at[n], g_rcv.at[n], (s, spot(k)))
+    def factor_x(k):
+        n = k - 1
+        return remote(ag.at[c, zh, x], ag.at[c, zh, x], g_snd.at[n], g_rcv.at[n], (s, spot(k)))
 
     def factor_z():
-        n = 2 * nx - 2
-        return remote(ag.at[c, zh, x], ag.at[c, zh, x], g_snd.at[n], g_rcv.at[n], opposite)
+        n = nx - 1
+        return remote(ag.at[c, zh], ag.at[c, zh], g_snd.at[n], g_rcv.at[n], opposite)
 
     def factor_c():
-        n = 2 * nx - 1
+        n = nx
         return remote(ag.at[c], ag.at[c], g_snd.at[n], g_rcv.at[n], partner)
 
     def store(j):
@@ -261,11 +260,10 @@
 
     b_load(0).wait()
     send_b(0)
-    factor_z().start()
     for z, dx in ((0, 2), (1, 2), (1, 1), (0, 3), (0, 1), (1, 3)):
         a_remote(z, dx).start()
     for k in range(1, nx):
-        factor_x(True, k).start()
+        factor_x(k).start()
     send_b2(0)
     for j in range(1, EARLY):
         b_load(j).wait()
@@ -463,17 +461,15 @@
                     tail_load(g, dx).wait()
                     tail_remote(g, dx).start()
 
-        @pl.when(i == 2)
+        @pl.when(i == 1)
+        def _():
+            for k in range(1, nx):
+                factor_x(k).wait_recv()
+            factor_z().start()
+
+        @pl.when(i == 1 + LAG)
         def _():
             factor_z().wait_recv()
-            for k in range(1, nx):
-                factor_x(False, k).start()
-
-        @pl.when(i == 3)
-        def _():
-            for k in range(1, nx):
-                factor_x(True, k).wait_recv()
-                factor_x(False, k).wait_recv()
             factor_c().start()
 
         for n, (low, high) in enumerate(PIECES2):
@@ -589,8 +585,7 @@
         for g in range(3):
             tail_remote(g, dx).wait_send()
     for k in range(1, nx):
-        factor_x(True, k).wait_send()
-        factor_x(False, k).wait_send()
+        factor_x(k).wait_send()
     factor_z().wait_send()
     factor_c().wait_send()
     lax.fori_loop(0, ns, drain, 0)
@@ -654,7 +649,7 @@
             dma((ns,)), dma((ns,)),
             dma((2, nc, SUBS)), dma((2, nc, SUBS)), dma((2, 2, nc)), dma((2, 2, nc)),
             dma((2, nu)), dma((2, nu)), dma((2, 2, nu)), dma((2, 2, nu)),
-            dma((nc,)), dma((nc,)), dma((2 * nx,)), dma((2 * nx,)), dma((nc,)), dma((ns,)),
+            dma((nc,)), dma((nc,)), dma((nx + 1,)), dma((nx + 1,)), dma((nc,)), dma((ns,)),
         ],
         compiler_params=pltpu.CompilerParams(
             collective_id=0, has_side_effects=True, vmem_limit_bytes=60 << 20

time: 118 us -> 115 us (0.975)
  Pallas kernels: 114 us -> 111 us
    pallas_call x1, Pallas kernels: 114 us -> 111 us  [local(): pl.pallas_call(functools.partial(kernel, dims), out_shape=jax.ShapeDtypeS...]
where the time goes in v5:
time: 115 us; the launch traced here: 113 us
  Pallas kernels  111 us (97%)
  local copies, waits for them, and re-layouts  2.65 us (2%)
    pallas_call x1, Pallas kernels, local(): pl.pallas_call(functools.partial(kernel, dims), out_shape=jax.ShapeDtypeS...  111 us
    unnamed x1, local copies, waits for them, and re-layouts  2.65 us

profile of v5, /device:TPU:0, one launch (start us, length us, event | category | flops | bytes accessed | tf_op | source)
XLA Modules:
  0.0 113.5 jit_solution(15187728936401931871)
XLA Ops:
  0.0 110.8 %shard_map.73 = bf16[1,512,1536]{2,1,0:T(8,128)(2,1)} custom-call(bf16[512,1536]{1,0:T(8,128)(2,1)} %emb.1, bf16[1,512,1536]{2,1,0:T(8,128)(2,1)} %hid.1, bf16[1,512,8192]{2,1,0:T(8,128)(2,1)} %og.1, s32[2,16]{1,0:T(2,128)} %bitcast.2, s32[1,12]{1,0:T(1,128)} %bitcast.3, bf16[1,4,128,128]{3,2,1,0:T(8,128)(2,1)} %ginv.1, bf16[1,1,2,128,128]{4,3,2,1,0:T(8,128)(2,1)} %ainv.1), custom_call_target="tpu_custom_call" | custom-call | flops 12884901888 | bytes 8388608 | tf_op jit(solution)/shard_map/pallas_call | solution.py:612
  110.8 2.7 %copy.9 = bf16[1,512,1536]{2,1,0:T(8,128)(2,1)} copy(bf16[1,512,1536]{2,1,0:T(8,128)(2,1)} %shard_map.73) | data formatting | bytes 3145728

commit v6 on v5

--- a/solution.py
+++ b/solution.py
@@ -497,7 +497,6 @@
                 wait_a((0, 0), (1, 0))
 
             away = term(j, (1 - zh) * nx)
-            mine = term(j, zh * nx)
             second(0, 1, j).wait_recv()
             second(1, 0, j).wait_recv()
             second(0, 0, j).wait_recv()
@@ -506,6 +505,7 @@
                 away + r2[0, 1 - zh, j].astype(F32) + r2[1, 1 - zh, j].astype(F32)
             ).astype(BF16)
             last(j).start()
+            mine = term(j, zh * nx)
             own[j] = mine + r2[0, zh, j].astype(F32) + r2[1, zh, j].astype(F32)
 
         @pl.when(i == nc + 1)

time: 115 us -> 115 us (level)
  no operation moved by 1% of the time
where the time goes in v6:
time: 115 us; the launch traced here: 113 us
  Pallas kernels  111 us (97%)
  local copies, waits for them, and re-layouts  2.65 us (2%)
    pallas_call x1, Pallas kernels, local(): pl.pallas_call(functools.partial(kernel, dims), out_shape=jax.ShapeDtypeS...  111 us
    unnamed x1, local copies, waits for them, and re-layouts  2.65 us

profile of v6, /device:TPU:0, one launch (start us, length us, event | category | flops | bytes accessed | tf_op | source)
XLA Modules:
  0.0 113.5 jit_solution(16181527161282873277)
XLA Ops:
  0.0 110.8 %shard_map.73 = bf16[1,512,1536]{2,1,0:T(8,128)(2,1)} custom-call(bf16[512,1536]{1,0:T(8,128)(2,1)} %emb.1, bf16[1,512,1536]{2,1,0:T(8,128)(2,1)} %hid.1, bf16[1,512,8192]{2,1,0:T(8,128)(2,1)} %og.1, s32[2,16]{1,0:T(2,128)} %bitcast.2, s32[1,12]{1,0:T(1,128)} %bitcast.3, bf16[1,4,128,128]{3,2,1,0:T(8,128)(2,1)} %ginv.1, bf16[1,1,2,128,128]{4,3,2,1,0:T(8,128)(2,1)} %ainv.1), custom_call_target="tpu_custom_call" | custom-call | flops 12884901888 | bytes 8388608 | tf_op jit(solution)/shard_map/pallas_call | solution.py:612
  110.8 2.7 %copy.9 = bf16[1,512,1536]{2,1,0:T(8,128)(2,1)} copy(bf16[1,512,1536]{2,1,0:T(8,128)(2,1)} %shard_map.73) | data formatting | bytes 3145728
